TPU v7x, 256 devices: a whole 4x4x8 slice. The times are simulated.
256 devices in a mesh: wide: 32 (over x, y, core), narrow: 8 (over z).
Axes of the slice: x: 4, y: 4, z: 8, core: 2. Of those that a mesh axis runs over, the one named last changes fastest.
Arguments:
- saved_codes: bfloat16 [768, 8192], P('wide', 'narrow'), may hold values from -4 to 4
- saved_scale: float32 [32, 8], P('wide', 'narrow'), may hold values from 0.5 to 2
- grad_output: bfloat16 [768, 8192], P('wide', 'narrow'), may hold values from -45 to 45
- gate_codes: bfloat16 [8192, 28672], P('narrow', 'wide'), may hold values from -0.0625 to 0.0625
- gate_scale: float32 [8, 32], P('narrow', 'wide'), may hold values from 0.5 to 2
- up_codes: bfloat16 [8192, 28672], P('narrow', 'wide'), may hold values from -0.0625 to 0.0625
- up_scale: float32 [8, 32], P('narrow', 'wide'), may hold values from 0.5 to 2
- down_codes: bfloat16 [28672, 8192], P('wide', 'narrow'), may hold values from -0.03125 to 0.03125
- down_scale: float32 [32, 8], P('wide', 'narrow'), may hold values from 0.5 to 2
Outputs:
- gate_out: bfloat16 [8192, 28672], P('narrow', 'wide')
- up_out: bfloat16 [8192, 28672], P('narrow', 'wide')
- down_out: bfloat16 [28672, 8192], P('wide', 'narrow')
- input_out: bfloat16 [768, 8192], P('wide', 'narrow')
- amaxes: float32 [4], replicated
All inputs are finite; a program needn't handle non-finite values. Where the computation divides by a largest or mean magnitude, that divisor is 1e-20 or more.
Results may differ from a plain program's by a relative error of at most 0.0079.
Values may be sent and summed in bfloat16 or wider, within the bound.
A program may use at most 128 MiB of HBM per device.

v0:
```python
import jax
import jax.numpy as jnp
from jax import lax
from jax.sharding import PartitionSpec as P

eps = 1e-06


def contract_last(left_mat, right_mat):
    return lax.dot_general(
        left_mat, right_mat, (((1,), (1,)), ((), ())), preferred_element_type=jnp.float32
    )


def contract_first(left_mat, right_mat):
    return lax.dot_general(
        left_mat, right_mat, (((0,), (0,)), ((), ())), preferred_element_type=jnp.float32
    )


def unit_grads(gate_pre, up_pre, hidden_grad):
    sigmoid_gate = jax.nn.sigmoid(gate_pre)
    silu_gate = gate_pre * sigmoid_gate
    hidden = (silu_gate * up_pre).astype(jnp.bfloat16)
    gate_grad = (
        hidden_grad * up_pre * sigmoid_gate * (1.0 + gate_pre * (1.0 - sigmoid_gate))
    ).astype(jnp.bfloat16)
    up_grad = (hidden_grad * silu_gate).astype(jnp.bfloat16)
    return (hidden, gate_grad, up_grad)


def largest(gradient):
    return jnp.max(jnp.abs(gradient))


def per_device(
    saved_codes,
    saved_scale,
    grad_output,
    gate_codes,
    gate_scale,
    up_codes,
    up_scale,
    down_codes,
    down_scale,
):
    saved = (saved_codes.astype(jnp.float32) * saved_scale).astype(jnp.bfloat16)
    saved_rows, grad_rows = (
        lax.all_gather(saved, "wide", axis=0, tiled=True),
        lax.all_gather(grad_output, "wide", axis=0, tiled=True),
    )
    gate_part = gate_scale[0, 0] * jnp.dot(
        saved_rows, gate_codes, preferred_element_type=jnp.float32
    )
    up_part = up_scale[0, 0] * jnp.dot(saved_rows, up_codes, preferred_element_type=jnp.float32)
    hidden_part = down_scale[0, 0] * contract_last(grad_rows, down_codes)
    gate_pre, up_pre, hidden_grad = lax.psum((gate_part, up_part, hidden_part), "narrow")
    hidden, gate_grad, up_grad = unit_grads(gate_pre, up_pre, hidden_grad)
    down_wgrad = contract_first(hidden, grad_rows)
    down_amax = lax.pmax(largest(down_wgrad), ("wide", "narrow")) + eps
    gate_wgrad = contract_first(saved_rows, gate_grad)
    up_wgrad = contract_first(saved_rows, up_grad)
    gate_amax, up_amax = lax.pmax((largest(gate_wgrad), largest(up_wgrad)), ("wide", "narrow"))
    gate_amax = gate_amax + eps
    up_amax = up_amax + eps
    input_grad = lax.psum_scatter(
        gate_scale[0, 0] * contract_last(gate_grad, gate_codes)
        + up_scale[0, 0] * contract_last(up_grad, up_codes),
        "wide",
        scatter_dimension=0,
        tiled=True,
    )
    input_amax = lax.pmax(largest(input_grad), ("wide", "narrow")) + eps
    gate_out = (gate_wgrad / gate_amax).astype(jnp.bfloat16)
    up_out = (up_wgrad / up_amax).astype(jnp.bfloat16)
    down_out = (down_wgrad / down_amax).astype(jnp.bfloat16)
    input_out = (input_grad / input_amax).astype(jnp.bfloat16)
    amaxes = jnp.stack([gate_amax, up_amax, down_amax, input_amax])
    return (gate_out, up_out, down_out, input_out, amaxes)


def solution(mesh):
    placed = (
        P("wide", "narrow"),
        P("wide", "narrow"),
        P("wide", "narrow"),
        P("narrow", "wide"),
        P("narrow", "wide"),
        P("narrow", "wide"),
        P("narrow", "wide"),
        P("wide", "narrow"),
        P("wide", "narrow"),
    )
    return jax.shard_map(
        per_device,
        mesh=mesh,
        in_specs=placed,
        out_specs=(
            P("narrow", "wide"),
            P("narrow", "wide"),
            P("wide", "narrow"),
            P("wide", "narrow"),
            P(),
        ),
        check_vma=False,
    )
```

profile of v0, /device:TPU:1, one launch (start us, length us, event | category | flops | bytes accessed | tf_op | source)
XLA Modules:
  0.0 498.4 jit_solution(14305283642889223144)
XLA Ops:
  8.0 1.4 multiply_convert_fusion.4
  9.5 0.0 all-gather.5.cloned.1.call-start
  9.5 0.7 all-gather.5.cloned.1.call-update
  12.2 51.5 %all-gather.3.cloned.1.call-done = bf16[768,1024]{1,0:T(8,128)(2,1)} async-done(((bf16[24,1024]{1,0:T(8,128)(2,1)}), bf16[768,1024]{1,0:T(8,128)(2,1)}) %all-gather.3.cloned.1.call-update) | async-done | bytes 1572880 | tf_op jit(solution)/shard_map/all_gather | solution.py:49
  63.7 4.9 convolution_multiply_fusion
  68.5 3.3 convolution_multiply_fusion.1
  71.9 42.0 %all-gather.5.cloned.1.call-done = bf16[768,1024]{1,0:T(8,128)(2,1)} async-done(((bf16[24,1024]{1,0:T(8,128)(2,1)}), bf16[768,1024]{1,0:T(8,128)(2,1)}) %all-gather.5.cloned.1.call-update) | async-done | bytes 1572880 | tf_op jit(solution)/shard_map/all_gather | solution.py:50
  113.9 5.4 %convolution_multiply_fusion.2 = f32[768,896]{1,0:T(8,128)} fusion(bf16[768,1024]{1,0:T(8,128)(2,1)} %all-gather.5.cloned.1.call-done, bf16[896,1024]{1,0:T(8,128)(2,1)} %param.16, f32[]{:T(128)} %bitcast.28), kind=kOutput, calls=%fused_computation.14 | convolution fusion | flops 1409974272 | bytes 6160388 | tf_op jit(solution)/shard_map/dot_general | solution.py:10
  119.3 0.2 reduce-scatter.2.cloned.1.call-start
  119.5 185.2 %all-reduce.4.cloned.1.call-done = (f32[768,896]{1,0:T(8,128)}, f32[768,896]{1,0:T(8,128)}, f32[768,896]{1,0:T(8,128)}) async-done(((f32[768,896]{1,0:T(8,128)}, f32[768,896]{1,0:T(8,128)}, f32[768,896]{1,0:T(8,128)}), (f32[768,896]{1,0:T(8,128)}, f32[768,896]{1,0:T(8,128)}, f32[768,896]{1,0:T(8,128)})) %all-reduce.4.cloned.1.call-update) | async-done | bytes 8257552 | tf_op jit(solution)/shard_map/psum | solution.py:57
  304.7 4.7 multiply_convert_fusion.1
  309.4 1.8 fusion.4
  311.3 0.2 copy-done.7
  311.4 3.6 multiply_add_fusion
  315.0 6.2 %abs_reduce_fusion.1 = (f32[]{:T(128)}, f32[1024,896]{1,0:T(8,128)}) fusion(bf16[768,1024]{1,0:T(8,128)(2,1)} %all-gather.3.cloned.1.call-done, bf16[768,896]{1,0:T(8,128)(2,1)} %copy-done.4), kind=kOutput, calls=%fused_computation.3 | convolution fusion | flops 1411121152 | bytes 6619140 | tf_op jit(solution)/shard_map/dot_general | solution.py:16
  321.2 4.3 abs_reduce_fusion.2
  325.5 4.2 abs_reduce_fusion
  329.8 70.6 %reduce-scatter.2.cloned.1.call-done = f32[24,1024]{1,0:T(8,128)} async-done(((f32[768,1024]{1,0:T(8,128)}), f32[24,1024]{1,0:T(8,128)}) %reduce-scatter.2.cloned.1.call-update) | async-done | bytes 98320 | tf_op jit(solution)/shard_map/reduce_scatter | solution.py:66
  400.4 1.5 abs_reduce_fusion.3
  401.9 77.4 %all-reduce = (f32[]{:T(128)}, f32[]{:T(128)}, f32[]{:T(128)}, f32[]{:T(128)}) all-reduce(f32[]{:T(128)} %get-tuple-element.14, f32[]{:T(128)} %get-tuple-element.16, f32[]{:T(128)} %get-tuple-element.18, f32[]{:T(128)} %abs_reduce_fusion.3), channel_id=1, replica_groups=mesh['wide'=32,'narrow'=8] {'wide','narrow'}, use_global_device_ids=true, to_apply=%region_4.0 | all-reduce | flops 4 | bytes 32 | tf_op jit(solution)/shard_map/pmax | solution.py:63
  481.9 3.9 divide_convert_fusion
  485.9 4.7 divide_convert_fusion.1
  490.6 0.6 pad_maximum_fusion
  491.2 0.6 divide_convert_fusion.3
  (26 shorter events, 0.2 us)
Async XLA Ops:
  7.2 56.5 %copy-start = (bf16[1024,896]{1,0:T(8,128)(2,1)S(1)}, bf16[1024,896]{1,0:T(8,128)(2,1)}, u32[]{:S(2)}) copy-start(bf16[1024,896]{1,0:T(8,128)(2,1)} %param.12) | copy-start | bytes 5505028
  7.2 56.5 %all-gather.3.cloned.1.call-start = ((), (), s32[]{:S(2)}) async-start(), calls=%async_computation.1 | async-start | bytes 1622016 | tf_op jit(solution)/shard_map/all_gather | solution.py:49
  9.5 104.4 %all-gather.5.cloned.1.call-start = ((), (), s32[]{:S(2)}) async-start(), calls=%async_computation.2 | async-start | bytes 1622016 | tf_op jit(solution)/shard_map/all_gather | solution.py:50
  10.2 294.5 %all-reduce.4.cloned.1.call-start = ((), (), s32[]{:S(2)}) async-start(), calls=%async_computation.4 | async-start | bytes 16515072 | tf_op jit(solution)/shard_map/psum | solution.py:57
  63.7 4.9 copy-start.6
  63.7 4.9 copy-start.8
  119.3 281.1 %reduce-scatter.2.cloned.1.call-start = ((), (), s32[]{:S(2)}) async-start(), calls=%async_computation.3 | async-start | bytes 3244032 | tf_op jit(solution)/shard_map/reduce_scatter | solution.py:66
  309.4 1.8 copy-start.4
  309.4 2.0 copy-start.7
  315.0 6.2 %copy-start.9 = (bf16[768,1024]{1,0:T(8,128)(2,1)S(1)}, bf16[768,1024]{1,0:T(8,128)(2,1)}, u32[]{:S(2)}) copy-start(bf16[768,1024]{1,0:T(8,128)(2,1)} %all-gather.3.cloned.1.call-done) | copy-start | bytes 4718596
  321.2 4.3 copy-start.2
  321.2 4.3 copy-start.3
  321.2 4.3 copy-start.10
  481.9 3.9 copy-start.1
  485.9 5.3 %copy-start.5 = (f32[24,1024]{1,0:T(8,128)S(1)}, f32[24,1024]{1,0:T(8,128)}, u32[]{:S(2)}) copy-start(f32[24,1024]{1,0:T(8,128)} %reduce-scatter.2.cloned.1.call-done) | copy-start | bytes 294916
Sparse Core Ops, SparseCore 0:
  11.1 52.4 all-gather.2
  66.2 47.6 all-gather.4
  119.4 185.2 all-reduce.3
  315.2 85.2 reduce-scatter.1
where the time goes:
time: 499 us; the launch traced here: 498 us
  waiting for transfers between devices  350 us (70%)
  blocking collectives  77.4 us (16%)
  matrix products  33.7 us (7%)
  between operations  19.1 us (4%)
  other arithmetic  17.5 us (4%)
    psum x1, waiting for transfers between devices, per_device(): lax.psum((gate_part, up_part, hidden_part), 'narrow')  185 us
    pmax x1, blocking collectives, per_device(): lax.pmax((largest(gate_wgrad), largest(up_wgrad)), ('wide', 'narrow'))  77.4 us
    reduce_scatter x1, waiting for transfers between devices, per_device(): lax.psum_scatter(gate_scale[0, 0] * contract_last(gate_grad, gate_codes)...  70.6 us
    all_gather x1, waiting for transfers between devices, per_device(): lax.all_gather(saved, 'wide', axis=0, tiled=True)  51.5 us
    all_gather x1, waiting for transfers between devices, per_device(): lax.all_gather(grad_output, 'wide', axis=0, tiled=True)  42 us
    dot_general x3, matrix products, contract_first(): lax.dot_general(left_mat, right_mat, (((0,), (0,)), ((), ())), preferred_...  14.7 us
    dot_general x3, matrix products, contract_last(): lax.dot_general(left_mat, right_mat, (((1,), (1,)), ((), ())), preferred_...  10.8 us
  transfers between devices with their start and end apart: 4, of which 4 were waited for; matrix products, arithmetic and copies ran while one was open for 5% of the time, Pallas kernels for 0%

commit v1 on v0

v1 whole, which is shorter than its diff:
```python
import jax
import jax.numpy as jnp
from jax import lax
from jax.experimental import pallas as pl
from jax.experimental.pallas import tpu as pltpu
from jax.sharding import PartitionSpec as P

eps = 1e-06
F32 = jnp.float32
BF16 = jnp.bfloat16
TOK, FEAT, UNIT = 768, 1024, 896
HALF = FEAT // 2
BLK = 48
CH = 96
NSEM = 200


def mm(lhs, rhs):
    return jnp.dot(lhs, rhs, preferred_element_type=F32)


def mm_last(lhs, rhs):
    return lax.dot_general(lhs, rhs, (((1,), (1,)), ((), ())), preferred_element_type=F32)


def mm_first(lhs, rhs):
    return lax.dot_general(lhs, rhs, (((0,), (0,)), ((), ())), preferred_element_type=F32)


def largest(value):
    rows, cols = value.shape
    folded = jnp.max(jnp.abs(value).reshape(rows // 8, 8, cols), axis=0)
    result = folded[:, :128]
    for start in range(128, cols, 128):
        result = jnp.maximum(result, folded[:, start : start + 128])
    return result


def kernel(
    saved_scale,
    gate_scale,
    up_scale,
    down_scale,
    saved_codes,
    grad_output,
    gate_hbm,
    up_hbm,
    down_hbm,
    gate_w,
    up_w,
    down_w,
    input_o,
    amax_o,
    X,
    W,
    DN,
    E,
    SE,
    RB,
    SB,
    H,
    PRE,
    IGK,
    IGS,
    CR,
    CS,
    RA,
    BS,
    RBB,
    FS,
    FIN,
    FX,
    MX,
    MR,
    send_sem,
    recv_sem,
    load_sem,
):
    wide = lax.axis_index("wide")
    z = lax.axis_index("narrow")
    core = lax.rem(wide, 2)
    x = wide // 8
    y = lax.rem(wide // 2, 4)
    a = x + core * (y - x)
    b = y + core * (x - y)

    def at(da, db):
        pa = lax.rem(a + da + 4, 4)
        pb = lax.rem(b + db + 4, 4)
        return pa + core * (pb - pa), pb + core * (pa - pb)

    def dev(da, db):
        px, py = at(da, db)
        return (px * 8 + py * 2 + core, z)

    def off(da, db):
        px, py = at(da, db)
        rel = lax.rem(px * 2 + py // 2 - z + 8, 8)
        far = rel // 4
        base = (1 - far) * (672 - 192 * rel) + far * 192 * (rel - 4)
        return pl.multiple_of(base + lax.rem(py, 2) * BLK, 16)

    partner = (wide + 1 - 2 * core, z)
    right = (wide, lax.rem(z + 1, 8))
    left = (wide, lax.rem(z + 7, 8))

    loads = []
    for arr, src in ((0, gate_hbm), (1, up_hbm)):
        for half in range(2):
            loads.append(
                pltpu.make_async_copy(
                    src.at[pl.ds(half * HALF, HALF)], W.at[arr, half], load_sem.at[len(loads)]
                )
            )
    loads.append(pltpu.make_async_copy(down_hbm, DN, load_sem.at[4]))
    for load in loads:
        load.start()

    barrier = pltpu.get_barrier_semaphore()
    others = [partner]
    others += [(wide, lax.rem(z + k, 8)) for k in range(1, 8)]
    others += [dev(k, 0) for k in range(1, 4)] + [dev(0, k) for k in range(1, 4)]
    for other in others:
        pl.semaphore_signal(barrier, inc=1, device_id=other, device_id_type=pl.DeviceIdType.MESH)

    started = []

    def send(src, dst, device):
        k = len(started)
        copy = pltpu.make_async_remote_copy(
            src_ref=src,
            dst_ref=dst,
            send_sem=send_sem.at[k],
            recv_sem=recv_sem.at[k],
            device_id=device,
            device_id_type=pl.DeviceIdType.MESH,
        )
        copy.start()
        started.append(copy)
        return copy

    first_core = core == 0
    tokens = [saved_codes[...].astype(F32) * saved_scale[0, 0], grad_output[...].astype(F32)]
    for t in range(2):
        low, high = tokens[t][:, :HALF], tokens[t][:, HALF:]
        E[t, core] = jnp.where(first_core, low, high)
        SE[t] = jnp.where(first_core, high, low)
    pl.semaphore_wait(barrier, len(others))
    swaps = [send(SE.at[t], E.at[t, core], partner) for t in range(2)]

    def gather(t):
        def full(da, db, device):
            ref = X.at[t, core, pl.ds(off(da, db), BLK)]
            return send(ref, ref, device)

        def part(da, db, q, device):
            ref = X.at[t, core, pl.ds(off(da, db), BLK), pl.ds(q * (HALF // 2), HALF // 2)]
            return send(ref, ref, device)

        swaps[t].wait_recv()
        X[t, core, pl.ds(off(0, 0), BLK)] = jnp.concatenate([E[t, 0], E[t, 1]], axis=0).astype(BF16)
        to_ap, to_am = full(0, 0, dev(1, 0)), full(0, 0, dev(-1, 0))
        bp, bm = [full(0, 0, dev(0, 1))], [full(0, 0, dev(0, -1))]
        pairs = [full(0, 0, partner)]
        yield
        order = [0, -1, 1, 2]
        to_ap.wait_recv()
        half_p = part(-1, 0, 0, dev(1, 0))
        bp.append(full(-1, 0, dev(0, 1)))
        bm.append(full(-1, 0, dev(0, -1)))
        pairs.append(full(-1, 0, partner))
        to_am.wait_recv()
        half_m = part(1, 0, 1, dev(-1, 0))
        bp.append(full(1, 0, dev(0, 1)))
        bm.append(full(1, 0, dev(0, -1)))
        pairs.append(full(1, 0, partner))
        yield
        half_p.wait_recv()
        half_m.wait_recv()
        bp.append(full(2, 0, dev(0, 1)))
        bm.append(full(2, 0, dev(0, -1)))
        pairs.append(full(2, 0, partner))
        yield
        hp, hm = [], []
        for i in range(4):
            bp[i].wait_recv()
            hp.append(part(order[i], -1, 0, dev(0, 1)))
            pairs.append(full(order[i], -1, partner))
            bm[i].wait_recv()
            hm.append(part(order[i], 1, 1, dev(0, -1)))
            pairs.append(full(order[i], 1, partner))
            if i % 2 == 1:
                yield
        for i in range(4):
            hp[i].wait_recv()
            hm[i].wait_recv()
            pairs.append(full(order[i], 2, partner))
        yield
        for pair in pairs:
            pair.wait_recv()

    def run(gen):
        for _ in gen:
            pass

    def step(gen):
        next(gen, None)

    run(gather(0))
    grads = gather(1)
    step(grads)

    scales = [gate_scale[0, 0], up_scale[0, 0], down_scale[0, 0]]

    def partial(arr, start, count):
        rows = pl.ds(start, count)
        if arr < 2:
            value = mm(X[0, 0, rows], W[arr, 0]) + mm(X[0, 1, rows], W[arr, 1])
        else:
            value = mm_last(X[1, 0, rows], DN[:, :HALF]) + mm_last(X[1, 1, rows], DN[:, HALF:])
        return value * scales[arr]

    def reduce(arr):
        def to_right(src, dst, count=CH):
            return send(SB.at[arr, pl.ds(src, count)], RB.at[arr, pl.ds(dst, count)], right)

        def to_left(src, dst, count=CH):
            return send(SB.at[arr, pl.ds(src, count)], RB.at[arr, pl.ds(dst, count)], left)

        SB[arr, 0:96] = partial(arr, 0, 96).astype(BF16)
        flow = [to_right(0, 96, BLK), to_left(48, 240, BLK)]
        yield
        value = partial(arr, 96, 192)
        SB[arr, 144:240] = value[48:144].astype(BF16)
        flow[0].wait_recv()
        SB[arr, 96:144] = (value[0:48] + RB[arr, 96:144].astype(F32)).astype(BF16)
        right_flow = to_right(96, 288)
        flow[1].wait_recv()
        SB[arr, 240:288] = (value[144:192] + RB[arr, 240:288].astype(F32)).astype(BF16)
        flow = [right_flow, to_left(192, 384)]
        yield
        for start in (288, 480):
            value = partial(arr, start, 192)
            flow[0].wait_recv()
            SB[arr, start : start + 96] = (value[:96] + RB[arr, start : start + 96].astype(F32)).astype(BF16)
            right_flow = to_right(start, start + 192)
            flow[1].wait_recv()
            SB[arr, start + 96 : start + 192] = (
                value[96:] + RB[arr, start + 96 : start + 192].astype(F32)
            ).astype(BF16)
            flow = [right_flow, to_left(start + 96, start + 288)]
            yield
        value = partial(arr, 672, 96)
        flow[0].wait_recv()
        flow[1].wait_recv()
        PRE[arr] = value + RB[arr, 672:768].astype(F32) + RB[arr, 768:864].astype(F32)
        yield

    def spread(arr):
        def to_right(src, dst, count=CH):
            return send(H.at[arr, pl.ds(src, count)], H.at[arr, pl.ds(dst, count)], right)

        def to_left(src, dst, count=CH):
            return send(H.at[arr, pl.ds(src, count)], H.at[arr, pl.ds(dst, count)], left)

        flow = [to_right(672, 576), to_left(672, 480)]
        yield
        flow[0].wait_recv()
        right_flow = to_right(576, 384)
        flow[1].wait_recv()
        flow = [right_flow, to_left(480, 288)]
        yield
        flow[0].wait_recv()
        right_flow = to_right(384, 192)
        flow[1].wait_recv()
        flow = [right_flow, to_left(288, 96)]
        yield
        flow[0].wait_recv()
        right_flow = to_right(192, 0, BLK)
        flow[1].wait_recv()
        flow = [right_flow, to_left(144, 48, BLK)]
        yield
        flow[0].wait_recv()
        flow[1].wait_recv()
        yield

    for load in loads[:4]:
        load.wait()
    gate_sum, up_sum, hidden_sum = reduce(0), reduce(1), reduce(2)
    for _ in range(3):
        step(gate_sum)
        step(grads)
        step(up_sum)
        step(grads)
    step(gate_sum)
    step(grads)
    step(up_sum)
    run(grads)
    loads[4].wait()
    step(hidden_sum)
    step(gate_sum)
    step(up_sum)

    def hidden_rows(i, carry):
        rows = pl.ds(pl.multiple_of(i * 16, 16), 16)
        gate_pre = PRE[0, rows]
        H[0, pl.ds(pl.multiple_of(672 + i * 16, 16), 16)] = (
            gate_pre * jax.nn.sigmoid(gate_pre) * PRE[1, rows]
        ).astype(BF16)
        return carry

    lax.fori_loop(0, 6, hidden_rows, 0)
    hidden_all, gate_all, up_all = spread(0), spread(1), spread(2)
    step(hidden_all)
    for _ in range(4):
        step(hidden_sum)

    def grad_rows(i, carry):
        rows = pl.ds(pl.multiple_of(i * 16, 16), 16)
        out = pl.ds(pl.multiple_of(672 + i * 16, 16), 16)
        gate_pre = PRE[0, rows]
        hidden_grad = PRE[2, rows]
        sig = jax.nn.sigmoid(gate_pre)
        H[1, out] = (hidden_grad * PRE[1, rows] * sig * (1.0 + gate_pre * (1.0 - sig))).astype(BF16)
        H[2, out] = (hidden_grad * gate_pre * sig).astype(BF16)
        return carry

    lax.fori_loop(0, 6, grad_rows, 0)
    step(gate_all)
    step(up_all)

    def weight_part(kind, start, count, first, last):
        def tile(i, top):
            rows = pl.ds(start, count)
            if kind < 2:
                ref = (gate_w, up_w)[kind]
                half = i // 2
                cols = pl.ds(pl.multiple_of(lax.rem(i, 2) * 256, 256), 256)
                value = mm_first(X[0, half, rows, cols], H[1 + kind, rows])
                where = pl.ds(pl.multiple_of(i * 256, 256), 256)
                if not first:
                    value = value + ref[where]
                ref[where] = value
            else:
                cols = pl.ds(pl.multiple_of(i * 128, 128), 128)
                value = jnp.concatenate(
                    [mm_first(H[0, rows, cols], X[1, half, rows]) for half in range(2)], axis=1
                )
                if not first:
                    value = value + down_w[cols]
                down_w[cols] = value
            return jnp.maximum(top, largest(value)) if last else top

        top = lax.fori_loop(0, 4 if kind < 2 else 7, tile, jnp.zeros((8, 128), F32))
        if last:
            MX[0, kind] = top

    pulls = []

    def input_part(start, count):
        rows = pl.ds(start, count)

        def half_value(half):
            return scales[0] * mm_last(H[1, rows], W[0, half]) + scales[1] * mm_last(H[2, rows], W[1, half])

        IGS[rows] = half_value(1 - core).astype(BF16)
        pulls.append(send(IGS.at[rows], CR.at[rows], partner))
        IGK[rows] = half_value(core)

    step(gate_all)
    step(up_all)
    input_part(480, 288)
    step(gate_all)
    step(up_all)
    input_part(288, 192)
    weight_part(0, 288, 480, True, False)
    step(gate_all)
    step(up_all)
    step(hidden_all)
    weight_part(1, 288, 480, True, False)
    input_part(96, 192)
    step(gate_all)
    step(up_all)
    input_part(0, 96)
    step(hidden_all)

    for pull in pulls:
        pull.wait_recv()
    across = []
    for da in range(1, 4):
        for db in range(4):
            rows = pl.ds(off(da, db), BLK)
            CS[da - 1, db] = (IGK[rows] + CR[rows].astype(F32)).astype(BF16)
        across.append(send(CS.at[da - 1], RA.at[da - 1], dev(da, 0)))
    weight_part(0, 96, 192, False, False)
    weight_part(1, 96, 192, False, False)
    step(hidden_all)
    weight_part(0, 0, 96, False, True)
    for copy in across:
        copy.wait_recv()
    along = []
    for db in (1, 2, 3, 0):
        rows = pl.ds(off(0, db), BLK)
        value = IGK[rows] + CR[rows].astype(F32)
        for k in range(3):
            value = value + RA[k, db].astype(F32)
        if db == 0:
            FS[...] = value
        else:
            BS[db - 1] = value.astype(BF16)
            along.append(send(BS.at[db - 1], RBB.at[db - 1], dev(0, db)))
    weight_part(1, 0, 96, False, True)
    weight_part(2, 288, 480, True, False)
    for copy in along:
        copy.wait_recv()
    value = FS[...]
    for k in range(3):
        value = value + RBB[k].astype(F32)
    FIN[0] = value[:24]
    FIN[1] = value[24:]
    last = send(FIN.at[1 - core], FX, partner)
    step(hidden_all)
    weight_part(2, 0, 288, False, True)
    last.wait_recv()
    mine, theirs = FIN[core], FX[...]
    low = jnp.where(first_core, mine, theirs)
    high = jnp.where(first_core, theirs, mine)
    input_o[:, :HALF] = low
    input_o[:, HALF:] = high
    MX[0, 3] = jnp.maximum(largest(low), largest(high))

    base = 0
    groups = [
        [(wide, lax.rem(z + k, 8)) for k in range(1, 8)],
        [dev(k, 0) for k in range(1, 4)],
        [dev(0, k) for k in range(1, 4)],
        [partner],
    ]
    for phase, group in enumerate(groups):
        copies = [send(MX.at[phase], MR.at[base + k], other) for k, other in enumerate(group)]
        value = MX[phase]
        for k, copy in enumerate(copies):
            copy.wait_recv()
            value = jnp.maximum(value, MR[base + k])
        MX[phase + 1] = value
        base += len(group)
    for k in range(4):
        amax_o[k : k + 1] = jnp.full((1, 128), jnp.max(MX[4, k]) + eps, F32)
    amax_o[4:] = jnp.zeros((4, 128), F32)

    for copy in started:
        copy.wait_send()


def per_device(
    saved_codes,
    saved_scale,
    grad_output,
    gate_codes,
    gate_scale,
    up_codes,
    up_scale,
    down_codes,
    down_scale,
):
    smem = pl.BlockSpec(memory_space=pltpu.SMEM)
    vmem = pl.BlockSpec(memory_space=pltpu.VMEM)
    hbm = pl.BlockSpec(memory_space=pl.ANY)
    gate_w, up_w, down_w, input_w, tops = pl.pallas_call(
        kernel,
        out_shape=[
            pltpu.VMEM((FEAT, UNIT), F32),
            pltpu.VMEM((FEAT, UNIT), F32),
            pltpu.VMEM((UNIT, FEAT), F32),
            pltpu.VMEM((24, FEAT), F32),
            pltpu.VMEM((8, 128), F32),
        ],
        in_specs=[smem] * 4 + [vmem] * 2 + [hbm] * 3,
        out_specs=[vmem] * 5,
        scratch_shapes=[
            pltpu.VMEM((2, 2, TOK, HALF), BF16),
            pltpu.VMEM((2, 2, HALF, UNIT), BF16),
            pltpu.VMEM((UNIT, FEAT), BF16),
            pltpu.VMEM((2, 2, 24, HALF), F32),
            pltpu.VMEM((2, 24, HALF), F32),
            pltpu.VMEM((3, 864, UNIT), BF16),
            pltpu.VMEM((3, 672, UNIT), BF16),
            pltpu.VMEM((3, TOK, UNIT), BF16),
            pltpu.VMEM((3, CH, UNIT), F32),
            pltpu.VMEM((TOK, HALF), F32),
            pltpu.VMEM((TOK, HALF), BF16),
            pltpu.VMEM((TOK, HALF), BF16),
            pltpu.VMEM((3, 4, BLK, HALF), BF16),
            pltpu.VMEM((3, 4, BLK, HALF), BF16),
            pltpu.VMEM((3, BLK, HALF), BF16),
            pltpu.VMEM((3, BLK, HALF), BF16),
            pltpu.VMEM((BLK, HALF), F32),
            pltpu.VMEM((2, 24, HALF), F32),
            pltpu.VMEM((24, HALF), F32),
            pltpu.VMEM((5, 4, 8, 128), F32),
            pltpu.VMEM((14, 4, 8, 128), F32),
            pltpu.SemaphoreType.DMA((NSEM,)),
            pltpu.SemaphoreType.DMA((NSEM,)),
            pltpu.SemaphoreType.DMA((5,)),
        ],
        compiler_params=pltpu.CompilerParams(
            collective_id=0, has_side_effects=True, vmem_limit_bytes=44 * 1024 * 1024
        ),
    )(
        saved_scale,
        gate_scale,
        up_scale,
        down_scale,
        saved_codes,
        grad_output,
        gate_codes,
        up_codes,
        down_codes,
    )
    gate_out = (gate_w / tops[0, 0]).astype(BF16)
    up_out = (up_w / tops[1, 0]).astype(BF16)
    down_out = (down_w / tops[2, 0]).astype(BF16)
    input_out = (input_w / tops[3, 0]).astype(BF16)
    return (gate_out, up_out, down_out, input_out, tops[:4, 0])


def solution(mesh):
    placed = (
        P("wide", "narrow"),
        P("wide", "narrow"),
        P("wide", "narrow"),
        P("narrow", "wide"),
        P("narrow", "wide"),
        P("narrow", "wide"),
        P("narrow", "wide"),
        P("wide", "narrow"),
        P("wide", "narrow"),
    )
    return jax.shard_map(
        per_device,
        mesh=mesh,
        in_specs=placed,
        out_specs=(
            P("narrow", "wide"),
            P("narrow", "wide"),
            P("wide", "narrow"),
            P("wide", "narrow"),
            P(),
        ),
        check_vma=False,
    )
```

time: 499 us -> 156 us (0.31)
  waiting for transfers between devices: 350 us -> 0 us
  Pallas kernels: 0 us -> 144 us
  blocking collectives: 77.4 us -> 0 us
  matrix products: 33.7 us -> 0 us
  between operations: 19.1 us -> 3.23 us
  other arithmetic: 17.5 us -> 7.24 us
    psum x1 -> x0, waiting for transfers between devices: 185 us -> none  [per_device(): lax.psum((gate_part, up_part, hidden_part), 'narrow')]
    pallas_call x0 -> x1, Pallas kernels: none -> 144 us  [per_device(): pl.pallas_call(kernel, out_shape=[pltpu.VMEM((FEAT, UNIT), F32), pltpu.VM...]
    all_gather x2 -> x0, waiting for transfers between devices: 93.5 us -> none  [the longest x1 51.5 us: per_device(): lax.all_gather(saved, 'wide', axis=0, tiled=True)]
    pmax x1 -> x0, blocking collectives: 77.4 us -> none  [per_device(): lax.pmax((largest(gate_wgrad), largest(up_wgrad)), ('wide', 'narrow'))]
    reduce_scatter x1 -> x0, waiting for transfers between devices: 70.6 us -> none  [per_device(): lax.psum_scatter(gate_scale[0, 0] * contract_last(gate_grad, gate_codes)...]
    dot_general x8 -> x0, matrix products: 33.7 us -> none  [the longest x3 14.7 us: contract_first(): lax.dot_general(left_mat, right_mat, (((0,), (0,)), ((), ())), preferred_...]
    convert_element_type x5 -> x3, other arithmetic: 15.4 us -> 7.24 us  [the longest x1 3.68 us: per_device(): up_out = (up_w / tops[1, 0]).astype(BF16)]
  transfers between devices with their start and end apart: 4 -> 0, of which waited for: 4 -> 0; matrix products, arithmetic and copies ran while one was open for 5% -> 0% of each run, Pallas kernels for 0% -> 0%
where the time goes in v1:
time: 156 us; the launch traced here: 155 us
  Pallas kernels  144 us (92%)
  other arithmetic  7.24 us (5%)
  between operations  3.23 us (2%)
    pallas_call x1, Pallas kernels, per_device(): pl.pallas_call(kernel, out_shape=[pltpu.VMEM((FEAT, UNIT), F32), pltpu.VM...  144 us
    convert_element_type x1, other arithmetic, per_device(): up_out = (up_w / tops[1, 0]).astype(BF16)  3.68 us

profile of v1, /device:TPU:1, one launch (start us, length us, event | category | flops | bytes accessed | tf_op | source)
XLA Modules:
  0.0 155.5 jit_solution(15743379710293980555)
XLA Ops:
  3.2 143.8 %shard_map.128 = (f32[1024,896]{1,0:T(8,128)S(1)}, f32[1024,896]{1,0:T(8,128)S(1)}, f32[896,1024]{1,0:T(8,128)S(1)}, f32[24,1024]{1,0:T(8,128)S(1)}, f32[8,128]{1,0:T(8,128)S(1)}) custom-call(f32[1,1]{1,0:T(1,128)S(6)} %copy.14.saved_scale, f32[1,1]{1,0:T(1,128)S(6)} %copy.15.gate_scale, f32[1,1]{1,0:T(1,128)S(6)} %copy.16.up_scale, ...), custom_call_target="tpu_custom_call" | custom-call | tf_op jit(solution)/shard_map/pallas_call | solution.py:469
  147.0 0.6 slice_reduce_fusion
  147.7 0.6 fusion
  148.2 3.7 %divide_convert_fusion.1 = (bf16[1024,896]{1,0:T(8,128)(2,1)}, bf16[1024,896]{1,0:T(8,128)(2,1)}) fusion(f32[1024,896]{1,0:T(8,128)S(1)} %get-tuple-element.12, f32[]{:T(128)} %bitcast.1, f32[1024,896]{1,0:T(8,128)S(1)} %get-tuple-element.10, f32[]{:T(128)} %bitcast), kind=kLoop, calls=%fused_computation.1 | loop fusion | flops 3670016 | bytes 11010056 | tf_op jit(solution)/shard_map/convert_element_type | solution.py:521
  151.9 2.4 %divide_convert_fusion = bf16[896,1024]{1,0:T(8,128)(2,1)} fusion(f32[896,1024]{1,0:T(8,128)S(1)} %get-tuple-element.13, f32[]{:T(128)} %bitcast.2), kind=kLoop, calls=%fused_computation | loop fusion | flops 1835008 | bytes 5505028 | tf_op jit(solution)/shard_map/convert_element_type | solution.py:522
  154.3 1.2 divide_convert_fusion.3

commit v2 on v1

v2 whole, which is shorter than its diff:
```python
import jax
import jax.numpy as jnp
from jax import lax
from jax.experimental import pallas as pl
from jax.experimental.pallas import tpu as pltpu
from jax.sharding import PartitionSpec as P

eps = 1e-06
F32 = jnp.float32
BF16 = jnp.bfloat16
TOK, FEAT, UNIT = 768, 1024, 896
HALF = FEAT // 2
BLK = 48
CH = 96
N_SEND, N_RECV = 21, 73


def mm(lhs, rhs):
    return jnp.dot(lhs, rhs, preferred_element_type=F32)


def mm_last(lhs, rhs):
    return lax.dot_general(lhs, rhs, (((1,), (1,)), ((), ())), preferred_element_type=F32)


def mm_first(lhs, rhs):
    return lax.dot_general(lhs, rhs, (((0,), (0,)), ((), ())), preferred_element_type=F32)


def largest(value):
    rows, cols = value.shape
    folded = jnp.max(jnp.abs(value).reshape(rows // 8, 8, cols), axis=0)
    result = folded[:, :128]
    for start in range(128, cols, 128):
        result = jnp.maximum(result, folded[:, start : start + 128])
    return result


def kernel(
    saved_scale,
    gate_scale,
    up_scale,
    down_scale,
    saved_codes,
    grad_output,
    gate_hbm,
    up_hbm,
    down_hbm,
    gate_o,
    up_o,
    down_o,
    input_o,
    amax_o,
    gate_w,
    up_w,
    down_w,
    X,
    W,
    DN,
    E,
    SE,
    RB,
    SB,
    H,
    PRE,
    IGK,
    IGS,
    CR,
    CS,
    RA,
    BS,
    RBB,
    FS,
    FIN,
    FX,
    IGO,
    MX,
    MR,
    send_sem,
    recv_sem,
    load_sem,
):
    wide = lax.axis_index("wide")
    z = lax.axis_index("narrow")
    core = lax.rem(wide, 2)
    x = wide // 8
    y = lax.rem(wide // 2, 4)
    a = x + core * (y - x)
    b = y + core * (x - y)

    def at(da, db):
        pa = lax.rem(a + da + 4, 4)
        pb = lax.rem(b + db + 4, 4)
        return pa + core * (pb - pa), pb + core * (pa - pb)

    def dev(da, db):
        px, py = at(da, db)
        return (px * 8 + py * 2 + core, z)

    def off(da, db):
        px, py = at(da, db)
        rel = lax.rem(px * 2 + py // 2 - z + 8, 8)
        far = rel // 4
        base = (1 - far) * (672 - 192 * rel) + far * 192 * (rel - 4)
        return pl.multiple_of(base + lax.rem(py, 2) * BLK, 16)

    partner = (wide + 1 - 2 * core, z)
    right = (wide, lax.rem(z + 1, 8))
    left = (wide, lax.rem(z + 7, 8))

    loads = []
    for arr, src in ((0, gate_hbm), (1, up_hbm)):
        for half in range(2):
            loads.append(
                pltpu.make_async_copy(
                    src.at[pl.ds(half * HALF, HALF)], W.at[arr, half], load_sem.at[len(loads)]
                )
            )
    loads.append(pltpu.make_async_copy(down_hbm, DN, load_sem.at[4]))
    for load in loads:
        load.start()

    barrier = pltpu.get_barrier_semaphore()
    others = [partner]
    others += [(wide, lax.rem(z + k, 8)) for k in range(1, 8)]
    others += [dev(k, j) for k in range(4) for j in range(4) if k + j > 0]
    for other in others:
        pl.semaphore_signal(barrier, inc=1, device_id=other, device_id_type=pl.DeviceIdType.MESH)

    used = {"send": 0, "recv": 0}
    finals = []

    def new(kind):
        used[kind] += 1
        return used[kind] - 1

    def remote(src, dst, to, sends, recvs):
        return pltpu.make_async_remote_copy(
            src_ref=src,
            dst_ref=dst,
            send_sem=send_sem.at[sends],
            recv_sem=recv_sem.at[recvs],
            device_id=to,
            device_id_type=pl.DeviceIdType.MESH,
        )

    class Batch:
        def __init__(self, total):
            self.sends = new("send")
            finals.append((total, self.sends))

        def send(self, src, dst, to, recvs):
            remote(src, dst, to, self.sends, recvs).start()

    def arrived(ref, recvs):
        remote(ref, ref, partner, 0, recvs).wait_recv()

    first_core = core == 0
    tokens = [saved_codes[...].astype(F32) * saved_scale[0, 0], grad_output[...].astype(F32)]
    for t in range(2):
        low, high = tokens[t][:, :HALF], tokens[t][:, HALF:]
        E[t, core] = jnp.where(first_core, low, high)
        SE[t] = jnp.where(first_core, high, low)
    pl.semaphore_wait(barrier, len(others))
    swap = Batch(SE)
    swaps = [new("recv") for _ in range(2)]
    for t in range(2):
        swap.send(SE.at[t], E.at[t, core], partner, swaps[t])

    def gather(t):
        plane = Batch(X.at[t, 0, pl.ds(0, 720)])
        pair = Batch(X.at[t, 0])
        pair_sem = new("recv")
        across = [new("recv") for _ in range(3)]
        along = [[new("recv") for _ in range(3)] for _ in range(4)]
        order = [0, 1, 3, 2]

        def block(da, db):
            return X.at[t, core, pl.ds(off(da, db), BLK)]

        def give(da, db):
            pair.send(block(da, db), block(da, db), partner, pair_sem)

        def give_along(i):
            for k in (1, 3, 2):
                plane.send(block(order[i], 0), block(order[i], 0), dev(0, k), along[i][k - 1])
            give(order[i], 0)

        arrived(E.at[t, 0], swaps[t])
        X[t, core, pl.ds(off(0, 0), BLK)] = jnp.concatenate([E[t, 0], E[t, 1]], axis=0).astype(BF16)
        for k in (1, 3, 2):
            plane.send(block(0, 0), block(0, 0), dev(k, 0), across[k - 1])
        give_along(0)
        yield
        for i in range(1, 4):
            arrived(block(0, 0), across[3 - order[i]])
            give_along(i)
            if i > 1:
                yield
        for i in range(4):
            for k in (1, 3, 2):
                arrived(block(0, 0), along[i][3 - k])
                give(order[i], k)
            if i % 2 == 1:
                yield
        arrived(X.at[t, 0], pair_sem)

    def run(gen):
        for _ in gen:
            pass

    def step(gen):
        next(gen, None)

    run(gather(0))
    grads = gather(1)
    step(grads)

    scales = [gate_scale[0, 0], up_scale[0, 0], down_scale[0, 0]]

    def partial(arr, start, count):
        rows = pl.ds(start, count)
        if arr < 2:
            value = mm(X[0, 0, rows], W[arr, 0]) + mm(X[0, 1, rows], W[arr, 1])
        else:
            value = mm_last(X[1, 0, rows], DN[:, :HALF]) + mm_last(X[1, 1, rows], DN[:, HALF:])
        return value * scales[arr]

    def reduce(arr):
        out = Batch(SB.at[arr])
        sems = [new("recv") for _ in range(4)]

        def push(k, src, dst_right, dst_left, count=CH):
            out.send(SB.at[arr, pl.ds(src, count)], RB.at[arr, pl.ds(dst_right, count)], right, sems[k])
            src = src + count
            out.send(SB.at[arr, pl.ds(src, count)], RB.at[arr, pl.ds(dst_left, count)], left, sems[k])

        SB[arr, 0:96] = partial(arr, 0, 96).astype(BF16)
        push(0, 0, 96, 240, BLK)
        yield
        value = partial(arr, 96, 192)
        arrived(RB.at[arr, pl.ds(0, 96)], sems[0])
        SB[arr, 96:144] = (value[0:48] + RB[arr, 96:144].astype(F32)).astype(BF16)
        SB[arr, 144:240] = value[48:144].astype(BF16)
        SB[arr, 240:288] = (value[144:192] + RB[arr, 240:288].astype(F32)).astype(BF16)
        push(1, 96, 288, 384)
        yield
        for k, start in ((2, 288), (3, 480)):
            value = partial(arr, start, 192)
            arrived(RB.at[arr, pl.ds(0, 192)], sems[k - 1])
            SB[arr, start : start + 192] = (value + RB[arr, start : start + 192].astype(F32)).astype(BF16)
            push(k, start, start + 192, start + 288)
            yield
        value = partial(arr, 672, 96)
        arrived(RB.at[arr, pl.ds(0, 192)], sems[3])
        PRE[arr] = value + RB[arr, 672:768].astype(F32) + RB[arr, 768:864].astype(F32)
        yield

    def spread(arr):
        out = Batch(H.at[arr, pl.ds(0, 672)])
        sems = [new("recv") for _ in range(4)]

        def push(k, src_right, dst_right, src_left, dst_left, count=CH):
            out.send(H.at[arr, pl.ds(src_right, count)], H.at[arr, pl.ds(dst_right, count)], right, sems[k])
            out.send(H.at[arr, pl.ds(src_left, count)], H.at[arr, pl.ds(dst_left, count)], left, sems[k])

        push(0, 672, 576, 672, 480)
        yield
        arrived(H.at[arr, pl.ds(0, 192)], sems[0])
        push(1, 576, 384, 480, 288)
        yield
        arrived(H.at[arr, pl.ds(0, 192)], sems[1])
        push(2, 384, 192, 288, 96)
        yield
        arrived(H.at[arr, pl.ds(0, 192)], sems[2])
        push(3, 192, 0, 144, 48, BLK)
        yield
        arrived(H.at[arr, pl.ds(0, 96)], sems[3])
        yield

    for load in loads[:4]:
        load.wait()
    gate_sum, up_sum, hidden_sum = reduce(0), reduce(1), reduce(2)
    for _ in range(3):
        step(gate_sum)
        step(grads)
        step(up_sum)
        step(grads)
    step(gate_sum)
    step(grads)
    step(up_sum)
    run(grads)
    loads[4].wait()
    step(hidden_sum)
    step(gate_sum)
    step(up_sum)

    def hidden_rows(i, carry):
        rows = pl.ds(pl.multiple_of(i * 16, 16), 16)
        gate_pre = PRE[0, rows]
        H[0, pl.ds(pl.multiple_of(672 + i * 16, 16), 16)] = (
            gate_pre * jax.nn.sigmoid(gate_pre) * PRE[1, rows]
        ).astype(BF16)
        return carry

    lax.fori_loop(0, 6, hidden_rows, 0)
    hidden_all, gate_all, up_all = spread(0), spread(1), spread(2)
    step(hidden_all)
    for _ in range(4):
        step(hidden_sum)

    def grad_rows(i, carry):
        rows = pl.ds(pl.multiple_of(i * 16, 16), 16)
        out = pl.ds(pl.multiple_of(672 + i * 16, 16), 16)
        gate_pre = PRE[0, rows]
        hidden_grad = PRE[2, rows]
        sig = jax.nn.sigmoid(gate_pre)
        H[1, out] = (hidden_grad * PRE[1, rows] * sig * (1.0 + gate_pre * (1.0 - sig))).astype(BF16)
        H[2, out] = (hidden_grad * gate_pre * sig).astype(BF16)
        return carry

    lax.fori_loop(0, 6, grad_rows, 0)
    step(gate_all)
    step(up_all)

    def set_top(which, k, top):
        MX[which, 0, 4 * k : 4 * k + 4] = jnp.maximum(top[:4], top[4:])

    def weight_part(kind, start, count, first, last):
        def tile(i, top):
            rows = pl.ds(start, count)
            if kind < 2:
                ref = (gate_w, up_w)[kind]
                half = i // 2
                cols = pl.ds(pl.multiple_of(lax.rem(i, 2) * 256, 256), 256)
                value = mm_first(X[0, half, rows, cols], H[1 + kind, rows])
                where = pl.ds(pl.multiple_of(i * 256, 256), 256)
                if not first:
                    value = value + ref[where]
                ref[where] = value
            else:
                cols = pl.ds(pl.multiple_of(i * 128, 128), 128)
                value = jnp.concatenate(
                    [mm_first(H[0, rows, cols], X[1, half, rows]) for half in range(2)], axis=1
                )
                if not first:
                    value = value + down_w[cols]
                down_w[cols] = value
            return jnp.maximum(top, largest(value)) if last else top

        top = lax.fori_loop(0, 4 if kind < 2 else 7, tile, jnp.zeros((8, 128), F32))
        if last:
            set_top(kind // 2, kind % 2, top)

    pulls = Batch(IGS)
    pull_sems = [new("recv") for _ in range(2)]
    across = Batch(CS.at[pl.ds(0, 12)])
    across_sems = [new("recv") for _ in range(3)]

    def input_part(start, count, batch):
        rows = pl.ds(start, count)

        def half_value(half):
            return scales[0] * mm_last(H[1, rows], W[0, half]) + scales[1] * mm_last(H[2, rows], W[1, half])

        IGS[rows] = half_value(1 - core).astype(BF16)
        pulls.send(IGS.at[rows], CR.at[rows], partner, pull_sems[batch])
        IGK[rows] = half_value(core)

    def input_across(lower, upper):
        def block(r, carry):
            q = r // 2
            odd = lax.rem(q, 2)
            rel = odd * ((7 - q) // 2) + (1 - odd) * (4 + q // 2)
            c = lax.rem(z + rel, 8)
            px = c // 2
            py = 2 * lax.rem(c, 2) + lax.rem(r, 2)
            da = lax.rem(px + core * (py - px) - a + 4, 4)
            db = lax.rem(py + core * (px - py) - b + 4, 4)

            @pl.when(da != 0)
            def _():
                rows = pl.ds(pl.multiple_of(r * BLK, 16), BLK)
                slot = (da - 1) * 4 + db
                CS[slot] = (IGK[rows] + CR[rows].astype(F32)).astype(BF16)
                for k in range(1, 4):
                    @pl.when(da == k)
                    def _():
                        across.send(CS.at[slot], RA.at[slot], dev(k, 0), across_sems[k - 1])

            return carry

        lax.fori_loop(lower, upper, block, 0)

    groups = [
        [partner],
        [(wide, lax.rem(z + k, 8)) for k in range(1, 8)],
        [dev(k, j) for k in range(4) for j in range(4) if k + j > 0],
    ]

    def maxima(which):
        base = 0
        for phase, group in enumerate(groups):
            out = Batch(MR.at[which, pl.ds(0, len(group))])
            sem = new("recv")
            for k, other in enumerate(group):
                out.send(MX.at[which, phase], MR.at[which, base + k], other, sem)
            yield
            arrived(MR.at[which, pl.ds(0, len(group))], sem)
            value = MX[which, phase]
            for k in range(len(group)):
                value = jnp.maximum(value, MR[which, base + k])
            MX[which, phase + 1] = value
            base += len(group)

    def amax(which, k):
        return jnp.max(MX[which, 3, 4 * k : 4 * k + 4]) + eps

    def scaled(src, dst, top):
        inverse = 1.0 / jnp.full((16, 128), top, F32)
        rows, cols = src.shape
        factor = jnp.concatenate([inverse] * (cols // 128), axis=1)

        def tile(i, carry):
            where = pl.ds(pl.multiple_of(i * 16, 16), 16)
            dst[where] = (src[where] * factor).astype(BF16)
            return carry

        lax.fori_loop(0, rows // 16, tile, 0)

    step(gate_all)
    step(up_all)
    input_part(480, 288, 0)
    step(gate_all)
    step(up_all)
    input_part(288, 192, 0)
    step(hidden_all)
    arrived(CR.at[pl.ds(0, 480)], pull_sems[0])
    input_across(6, 16)
    weight_part(0, 288, 480, True, False)
    step(gate_all)
    step(up_all)
    input_part(96, 192, 1)
    step(hidden_all)
    weight_part(1, 288, 480, True, False)
    step(gate_all)
    step(up_all)
    input_part(0, 96, 1)
    step(hidden_all)
    weight_part(0, 0, 288, False, True)
    arrived(CR.at[pl.ds(0, 288)], pull_sems[1])
    input_across(0, 6)
    weight_part(1, 0, 288, False, True)
    first_tops = maxima(0)
    step(first_tops)
    weight_part(2, 288, 480, True, False)
    step(first_tops)
    for sem in across_sems:
        arrived(RA.at[pl.ds(0, 4)], sem)
    along = Batch(BS)
    along_sems = [new("recv") for _ in range(3)]
    for db in (2, 1, 3, 0):
        rows = pl.ds(off(0, db), BLK)
        value = IGK[rows] + CR[rows].astype(F32)
        for k in range(3):
            value = value + RA[4 * k + db].astype(F32)
        if db == 0:
            FS[...] = value
        else:
            BS[db - 1] = value.astype(BF16)
            along.send(BS.at[db - 1], RBB.at[db - 1], dev(0, db), along_sems[db - 1])
    step(hidden_all)
    step(first_tops)
    weight_part(2, 0, 288, False, True)
    value = FS[...]
    for k in range(3):
        arrived(RBB.at[0], along_sems[k])
        value = value + RBB[k].astype(F32)
    FIN[0] = value[:24]
    FIN[1] = value[24:]
    last = Batch(FX)
    last_sem = new("recv")
    last.send(FIN.at[1 - core], FX, partner, last_sem)
    run(first_tops)
    arrived(FX, last_sem)
    mine, theirs = FIN[core], FX[...]
    low = jnp.where(first_core, mine, theirs)
    high = jnp.where(first_core, theirs, mine)
    IGO[:, :HALF] = low
    IGO[:, HALF:] = high
    set_top(1, 1, jnp.maximum(largest(low), largest(high)))
    second_tops = maxima(1)
    step(second_tops)
    step(second_tops)
    scaled(gate_w, gate_o, amax(0, 0))
    step(second_tops)
    scaled(up_w, up_o, amax(0, 1))
    run(second_tops)
    scaled(down_w, down_o, amax(1, 0))
    inverse = 1.0 / jnp.full((24, 128), amax(1, 1), F32)
    input_o[...] = (IGO[...] * jnp.concatenate([inverse] * 8, axis=1)).astype(BF16)
    for k in range(4):
        amax_o[k : k + 1] = jnp.full((1, 128), amax(k // 2, k % 2), F32)
    amax_o[4:] = jnp.zeros((4, 128), F32)

    assert (used["send"], used["recv"]) == (N_SEND, N_RECV), used
    for total, sends in finals:
        remote(total, total, partner, sends, 0).wait_send()


def per_device(
    saved_codes,
    saved_scale,
    grad_output,
    gate_codes,
    gate_scale,
    up_codes,
    up_scale,
    down_codes,
    down_scale,
):
    smem = pl.BlockSpec(memory_space=pltpu.SMEM)
    vmem = pl.BlockSpec(memory_space=pltpu.VMEM)
    hbm = pl.BlockSpec(memory_space=pl.ANY)
    gate_out, up_out, down_out, input_out, tops = pl.pallas_call(
        kernel,
        out_shape=[
            pltpu.VMEM((FEAT, UNIT), BF16),
            pltpu.VMEM((FEAT, UNIT), BF16),
            pltpu.VMEM((UNIT, FEAT), BF16),
            pltpu.VMEM((24, FEAT), BF16),
            pltpu.VMEM((8, 128), F32),
        ],
        in_specs=[smem] * 4 + [vmem] * 2 + [hbm] * 3,
        out_specs=[vmem] * 5,
        scratch_shapes=[
            pltpu.VMEM((FEAT, UNIT), F32),
            pltpu.VMEM((FEAT, UNIT), F32),
            pltpu.VMEM((UNIT, FEAT), F32),
            pltpu.VMEM((2, 2, TOK, HALF), BF16),
            pltpu.VMEM((2, 2, HALF, UNIT), BF16),
            pltpu.VMEM((UNIT, FEAT), BF16),
            pltpu.VMEM((2, 2, 24, HALF), F32),
            pltpu.VMEM((2, 24, HALF), F32),
            pltpu.VMEM((3, 864, UNIT), BF16),
            pltpu.VMEM((3, 672, UNIT), BF16),
            pltpu.VMEM((3, TOK, UNIT), BF16),
            pltpu.VMEM((3, CH, UNIT), F32),
            pltpu.VMEM((TOK, HALF), F32),
            pltpu.VMEM((TOK, HALF), BF16),
            pltpu.VMEM((TOK, HALF), BF16),
            pltpu.VMEM((12, BLK, HALF), BF16),
            pltpu.VMEM((12, BLK, HALF), BF16),
            pltpu.VMEM((3, BLK, HALF), BF16),
            pltpu.VMEM((3, BLK, HALF), BF16),
            pltpu.VMEM((BLK, HALF), F32),
            pltpu.VMEM((2, 24, HALF), F32),
            pltpu.VMEM((24, HALF), F32),
            pltpu.VMEM((24, FEAT), F32),
            pltpu.VMEM((2, 4, 8, 128), F32),
            pltpu.VMEM((2, 23, 8, 128), F32),
            pltpu.SemaphoreType.DMA((N_SEND,)),
            pltpu.SemaphoreType.DMA((N_RECV,)),
            pltpu.SemaphoreType.DMA((5,)),
        ],
        compiler_params=pltpu.CompilerParams(
            collective_id=0, has_side_effects=True, vmem_limit_bytes=52 * 1024 * 1024
        ),
    )(
        saved_scale,
        gate_scale,
        up_scale,
        down_scale,
        saved_codes,
        grad_output,
        gate_codes,
        up_codes,
        down_codes,
    )
    return (gate_out, up_out, down_out, input_out, tops[:4, 0])


def solution(mesh):
    placed = (
        P("wide", "narrow"),
        P("wide", "narrow"),
        P("wide", "narrow"),
        P("narrow", "wide"),
        P("narrow", "wide"),
        P("narrow", "wide"),
        P("narrow", "wide"),
        P("wide", "narrow"),
        P("wide", "narrow"),
    )
    return jax.shard_map(
        per_device,
        mesh=mesh,
        in_specs=placed,
        out_specs=(
            P("narrow", "wide"),
            P("narrow", "wide"),
            P("wide", "narrow"),
            P("wide", "narrow"),
            P(),
        ),
        check_vma=False,
    )
```

time: 156 us -> 146 us (0.936)
  other arithmetic: 7.24 us -> 0 us
  Pallas kernels: 144 us -> 138 us
  local copies, waits for them, and re-layouts: 1.18 us -> 4.93 us
    convert_element_type x3 -> x0, other arithmetic: 7.24 us -> none  [the longest x1 3.68 us: per_device(): up_out = (up_w / tops[1, 0]).astype(BF16)]
    pallas_call x1, Pallas kernels: 144 us -> 138 us  [per_device(): pl.pallas_call(kernel, out_shape=[pltpu.VMEM((FEAT, UNIT), BF16), pltpu.V...]
    unnamed x0 -> x4, local copies, waits for them, and re-layouts: none -> 4.31 us
where the time goes in v2:
time: 146 us
  Pallas kernels  138 us (95%)
  local copies, waits for them, and re-layouts  4.93 us (3%)
  between operations  3.23 us (2%)
    pallas_call x1, Pallas kernels, per_device(): pl.pallas_call(kernel, out_shape=[pltpu.VMEM((FEAT, UNIT), BF16), pltpu.V...  138 us
    unnamed x4, local copies, waits for them, and re-layouts  4.31 us

profile of v2, /device:TPU:1, one launch (start us, length us, event | category | flops | bytes accessed | tf_op | source)
XLA Modules:
  0.0 146.2 jit_solution(2022042478161453642)
XLA Ops:
  3.2 138.0 %shard_map.128 = (bf16[1024,896]{1,0:T(8,128)(2,1)S(1)}, bf16[1024,896]{1,0:T(8,128)(2,1)S(1)}, bf16[896,1024]{1,0:T(8,128)(2,1)S(1)}, bf16[24,1024]{1,0:T(8,128)(2,1)S(1)}, f32[8,128]{1,0:T(8,128)S(1)}) custom-call(f32[1,1]{1,0:T(1,128)S(6)} %copy.22.saved_scale, f32[1,1]{1,0:T(1,128)S(6)} %copy.23.gate_scale, f32[1,1]{1,0:T(1,128)S(6)} %copy.24.up_scale, ...), custom_call_target="tpu_custom_call" | custom-call | tf_op jit(solution)/shard_map/pallas_call | solution.py:525
  141.2 1.2 copy.18
  142.5 0.6 slice_reduce_fusion
  143.1 0.6 copy.21
  143.7 1.2 copy.19
  145.0 1.2 copy.20

commit v3 on v2

--- a/solution.py
+++ b/solution.py
@@ -12,7 +12,8 @@
 HALF = FEAT // 2
 BLK = 48
 CH = 96
-N_SEND, N_RECV = 21, 73
+WINDOW = 9
+N_SEND, N_RECV = 15 + WINDOW, 73
 
 
 def mm(lhs, rhs):
@@ -61,8 +62,11 @@
     SE,
     RB,
     SB,
+    RF,
+    SF,
     H,
     PRE,
+    AHEAD,
     IGK,
     IGS,
     CR,
@@ -152,6 +156,22 @@
         def send(self, src, dst, to, recvs):
             remote(src, dst, to, self.sends, recvs).start()
 
+    z_free = [new("send") for _ in range(WINDOW)]
+    z_last = []
+
+    def z_left(most):
+        while len(z_last) > most:
+            ref, sem = z_last.pop(0)
+            remote(ref, ref, partner, sem, 0).wait_send()
+            z_free.append(sem)
+
+    def z_push(total, to_right, to_left, recvs):
+        z_left(WINDOW - 1)
+        sem = z_free.pop(0)
+        remote(*to_right, right, sem, recvs).start()
+        remote(*to_left, left, sem, recvs).start()
+        z_last.append((total, sem))
+
     def arrived(ref, recvs):
         remote(ref, ref, partner, 0, recvs).wait_recv()
 
@@ -227,42 +247,61 @@
         return value * scales[arr]
 
     def reduce(arr):
-        out = Batch(SB.at[arr])
         sems = [new("recv") for _ in range(4)]
 
         def push(k, src, dst_right, dst_left, count=CH):
-            out.send(SB.at[arr, pl.ds(src, count)], RB.at[arr, pl.ds(dst_right, count)], right, sems[k])
-            src = src + count
-            out.send(SB.at[arr, pl.ds(src, count)], RB.at[arr, pl.ds(dst_left, count)], left, sems[k])
+            z_push(
+                SB.at[arr, pl.ds(src, 2 * count)],
+                (SB.at[arr, pl.ds(src, count)], RB.at[arr, pl.ds(dst_right, count)]),
+                (SB.at[arr, pl.ds(src + count, count)], RB.at[arr, pl.ds(dst_left, count)]),
+                sems[k],
+            )
 
         SB[arr, 0:96] = partial(arr, 0, 96).astype(BF16)
         push(0, 0, 96, 240, BLK)
         yield
-        value = partial(arr, 96, 192)
+        if arr == 0:
+            for start, count in ((96, 192), (288, 192), (480, 192), (672, 96)):
+                AHEAD[start - 96 : start - 96 + count] = partial(arr, start, count)
+            yield
+
+        def part(start, count):
+            return AHEAD[start - 96 : start - 96 + count] if arr == 0 else partial(arr, start, count)
+
+        value = part(96, 192)
         arrived(RB.at[arr, pl.ds(0, 96)], sems[0])
         SB[arr, 96:144] = (value[0:48] + RB[arr, 96:144].astype(F32)).astype(BF16)
         SB[arr, 144:240] = value[48:144].astype(BF16)
         SB[arr, 240:288] = (value[144:192] + RB[arr, 240:288].astype(F32)).astype(BF16)
         push(1, 96, 288, 384)
         yield
-        for k, start in ((2, 288), (3, 480)):
-            value = partial(arr, start, 192)
-            arrived(RB.at[arr, pl.ds(0, 192)], sems[k - 1])
-            SB[arr, start : start + 192] = (value + RB[arr, start : start + 192].astype(F32)).astype(BF16)
-            push(k, start, start + 192, start + 288)
+        for k, start, got in ((2, 288, RB.at[arr, 288:480]), (3, 480, RF.at[arr, 0:192])):
+            value = part(start, 192)
+            arrived(got, sems[k - 1])
+            src = start - 288
+            SF[arr, src : src + 192] = value + got[...].astype(F32)
+            z_push(
+                SF.at[arr, pl.ds(src, 192)],
+                (SF.at[arr, pl.ds(src, CH)], RF.at[arr, pl.ds(src, CH)]),
+                (SF.at[arr, pl.ds(src + CH, CH)], RF.at[arr, pl.ds(src + CH, CH)]),
+                sems[k],
+            )
             yield
-        value = partial(arr, 672, 96)
-        arrived(RB.at[arr, pl.ds(0, 192)], sems[3])
-        PRE[arr] = value + RB[arr, 672:768].astype(F32) + RB[arr, 768:864].astype(F32)
+        value = part(672, 96)
+        arrived(RF.at[arr, 192:384], sems[3])
+        PRE[arr] = value + RF[arr, 192:288] + RF[arr, 288:384]
         yield
 
     def spread(arr):
-        out = Batch(H.at[arr, pl.ds(0, 672)])
         sems = [new("recv") for _ in range(4)]
 
         def push(k, src_right, dst_right, src_left, dst_left, count=CH):
-            out.send(H.at[arr, pl.ds(src_right, count)], H.at[arr, pl.ds(dst_right, count)], right, sems[k])
-            out.send(H.at[arr, pl.ds(src_left, count)], H.at[arr, pl.ds(dst_left, count)], left, sems[k])
+            z_push(
+                H.at[arr, pl.ds(0, 2 * count)],
+                (H.at[arr, pl.ds(src_right, count)], H.at[arr, pl.ds(dst_right, count)]),
+                (H.at[arr, pl.ds(src_left, count)], H.at[arr, pl.ds(dst_left, count)]),
+                sems[k],
+            )
 
         push(0, 672, 576, 672, 480)
         yield
@@ -281,16 +320,22 @@
     for load in loads[:4]:
         load.wait()
     gate_sum, up_sum, hidden_sum = reduce(0), reduce(1), reduce(2)
-    for _ in range(3):
-        step(gate_sum)
-        step(grads)
-        step(up_sum)
-        step(grads)
+    step(gate_sum)
+    step(gate_sum)
+    step(up_sum)
     step(gate_sum)
     step(grads)
     step(up_sum)
+    step(grads)
+    step(grads)
+    step(gate_sum)
     run(grads)
     loads[4].wait()
+    step(hidden_sum)
+    step(up_sum)
+    step(hidden_sum)
+    step(gate_sum)
+    step(up_sum)
     step(hidden_sum)
     step(gate_sum)
     step(up_sum)
@@ -306,22 +351,30 @@
     lax.fori_loop(0, 6, hidden_rows, 0)
     hidden_all, gate_all, up_all = spread(0), spread(1), spread(2)
     step(hidden_all)
-    for _ in range(4):
-        step(hidden_sum)
-
-    def grad_rows(i, carry):
+    step(hidden_sum)
+    step(hidden_all)
+    step(hidden_sum)
+
+    def gate_rows(i, carry):
         rows = pl.ds(pl.multiple_of(i * 16, 16), 16)
-        out = pl.ds(pl.multiple_of(672 + i * 16, 16), 16)
         gate_pre = PRE[0, rows]
-        hidden_grad = PRE[2, rows]
         sig = jax.nn.sigmoid(gate_pre)
-        H[1, out] = (hidden_grad * PRE[1, rows] * sig * (1.0 + gate_pre * (1.0 - sig))).astype(BF16)
-        H[2, out] = (hidden_grad * gate_pre * sig).astype(BF16)
+        H[1, pl.ds(pl.multiple_of(672 + i * 16, 16), 16)] = (
+            PRE[2, rows] * PRE[1, rows] * sig * (1.0 + gate_pre * (1.0 - sig))
+        ).astype(BF16)
         return carry
 
-    lax.fori_loop(0, 6, grad_rows, 0)
+    def up_rows(i, carry):
+        rows = pl.ds(pl.multiple_of(i * 16, 16), 16)
+        gate_pre = PRE[0, rows]
+        H[2, pl.ds(pl.multiple_of(672 + i * 16, 16), 16)] = (
+            PRE[2, rows] * gate_pre * jax.nn.sigmoid(gate_pre)
+        ).astype(BF16)
+        return carry
+
+    lax.fori_loop(0, 6, gate_rows, 0)
     step(gate_all)
-    step(up_all)
+    lax.fori_loop(0, 6, up_rows, 0)
 
     def set_top(which, k, top):
         MX[which, 0, 4 * k : 4 * k + 4] = jnp.maximum(top[:4], top[4:])
@@ -428,20 +481,20 @@
 
         lax.fori_loop(0, rows // 16, tile, 0)
 
+    weight_part(2, 480, 288, True, False)
+    step(up_all)
     step(gate_all)
     step(up_all)
     input_part(480, 288, 0)
     step(gate_all)
     step(up_all)
     input_part(288, 192, 0)
-    step(hidden_all)
+    weight_part(0, 288, 480, True, False)
     arrived(CR.at[pl.ds(0, 480)], pull_sems[0])
     input_across(6, 16)
-    weight_part(0, 288, 480, True, False)
     step(gate_all)
     step(up_all)
     input_part(96, 192, 1)
-    step(hidden_all)
     weight_part(1, 288, 480, True, False)
     step(gate_all)
     step(up_all)
@@ -451,9 +504,10 @@
     arrived(CR.at[pl.ds(0, 288)], pull_sems[1])
     input_across(0, 6)
     weight_part(1, 0, 288, False, True)
+    step(hidden_all)
     first_tops = maxima(0)
     step(first_tops)
-    weight_part(2, 288, 480, True, False)
+    weight_part(2, 288, 192, False, False)
     step(first_tops)
     for sem in across_sems:
         arrived(RA.at[pl.ds(0, 4)], sem)
@@ -470,7 +524,6 @@
             BS[db - 1] = value.astype(BF16)
             along.send(BS.at[db - 1], RBB.at[db - 1], dev(0, db), along_sems[db - 1])
     step(hidden_all)
-    step(first_tops)
     weight_part(2, 0, 288, False, True)
     value = FS[...]
     for k in range(3):
@@ -478,23 +531,22 @@
         value = value + RBB[k].astype(F32)
     FIN[0] = value[:24]
     FIN[1] = value[24:]
+    set_top(1, 1, largest(value))
+    second_tops = maxima(1)
+    step(second_tops)
     last = Batch(FX)
     last_sem = new("recv")
     last.send(FIN.at[1 - core], FX, partner, last_sem)
+    step(second_tops)
+    step(first_tops)
     run(first_tops)
-    arrived(FX, last_sem)
-    mine, theirs = FIN[core], FX[...]
-    low = jnp.where(first_core, mine, theirs)
-    high = jnp.where(first_core, theirs, mine)
-    IGO[:, :HALF] = low
-    IGO[:, HALF:] = high
-    set_top(1, 1, jnp.maximum(largest(low), largest(high)))
-    second_tops = maxima(1)
-    step(second_tops)
-    step(second_tops)
     scaled(gate_w, gate_o, amax(0, 0))
     step(second_tops)
     scaled(up_w, up_o, amax(0, 1))
+    arrived(FX, last_sem)
+    mine, theirs = FIN[core], FX[...]
+    IGO[:, :HALF] = jnp.where(first_core, mine, theirs)
+    IGO[:, HALF:] = jnp.where(first_core, theirs, mine)
     run(second_tops)
     scaled(down_w, down_o, amax(1, 0))
     inverse = 1.0 / jnp.full((24, 128), amax(1, 1), F32)
@@ -503,6 +555,7 @@
         amax_o[k : k + 1] = jnp.full((1, 128), amax(k // 2, k % 2), F32)
     amax_o[4:] = jnp.zeros((4, 128), F32)
 
+    z_left(0)
     assert (used["send"], used["recv"]) == (N_SEND, N_RECV), used
     for total, sends in finals:
         remote(total, total, partner, sends, 0).wait_send()
@@ -542,10 +595,13 @@
             pltpu.VMEM((UNIT, FEAT), BF16),
             pltpu.VMEM((2, 2, 24, HALF), F32),
             pltpu.VMEM((2, 24, HALF), F32),
-            pltpu.VMEM((3, 864, UNIT), BF16),
-            pltpu.VMEM((3, 672, UNIT), BF16),
+            pltpu.VMEM((3, 480, UNIT), BF16),
+            pltpu.VMEM((3, 288, UNIT), BF16),
+            pltpu.VMEM((3, 384, UNIT), F32),
+            pltpu.VMEM((3, 384, UNIT), F32),
             pltpu.VMEM((3, TOK, UNIT), BF16),
             pltpu.VMEM((3, CH, UNIT), F32),
+            pltpu.VMEM((672, UNIT), F32),
             pltpu.VMEM((TOK, HALF), F32),
             pltpu.VMEM((TOK, HALF), BF16),
             pltpu.VMEM((TOK, HALF), BF16),
@@ -564,7 +620,7 @@
             pltpu.SemaphoreType.DMA((5,)),
         ],
         compiler_params=pltpu.CompilerParams(
-            collective_id=0, has_side_effects=True, vmem_limit_bytes=52 * 1024 * 1024
+            collective_id=0, has_side_effects=True, vmem_limit_bytes=54 * 1024 * 1024
         ),
     )(
         saved_scale,

time: 146 us -> 155 us (1.062)
  Pallas kernels: 138 us -> 147 us
    pallas_call x1, Pallas kernels: 138 us -> 147 us  [per_device(): pl.pallas_call(kernel, out_shape=[pltpu.VMEM((FEAT, UNIT), BF16), pltpu.V...]
where the time goes in v3:
time: 155 us
  Pallas kernels  147 us (95%)
  local copies, waits for them, and re-layouts  4.93 us (3%)
  between operations  3.23 us (2%)
    pallas_call x1, Pallas kernels, per_device(): pl.pallas_call(kernel, out_shape=[pltpu.VMEM((FEAT, UNIT), BF16), pltpu.V...  147 us
    unnamed x4, local copies, waits for them, and re-layouts  4.31 us

profile of v3, /device:TPU:1, one launch (start us, length us, event | category | flops | bytes accessed | tf_op | source)
XLA Modules:
  0.0 155.1 jit_solution(11368022505203163507)
XLA Ops:
  3.2 146.9 %shard_map.128 = (bf16[1024,896]{1,0:T(8,128)(2,1)S(1)}, bf16[1024,896]{1,0:T(8,128)(2,1)S(1)}, bf16[896,1024]{1,0:T(8,128)(2,1)S(1)}, bf16[24,1024]{1,0:T(8,128)(2,1)S(1)}, f32[8,128]{1,0:T(8,128)S(1)}) custom-call(f32[1,1]{1,0:T(1,128)S(6)} %copy.22.saved_scale, f32[1,1]{1,0:T(1,128)S(6)} %copy.23.gate_scale, f32[1,1]{1,0:T(1,128)S(6)} %copy.24.up_scale, ...), custom_call_target="tpu_custom_call" | custom-call | tf_op jit(solution)/shard_map/pallas_call | solution.py:578
  150.1 1.2 copy.18
  151.4 0.6 slice_reduce_fusion
  152.0 0.6 copy.21
  152.6 1.2 copy.19
  153.8 1.2 copy.20

commit v4 on v3

--- a/solution.py
+++ b/solution.py
@@ -275,21 +275,24 @@
         SB[arr, 240:288] = (value[144:192] + RB[arr, 240:288].astype(F32)).astype(BF16)
         push(1, 96, 288, 384)
         yield
-        for k, start, got in ((2, 288, RB.at[arr, 288:480]), (3, 480, RF.at[arr, 0:192])):
-            value = part(start, 192)
-            arrived(got, sems[k - 1])
-            src = start - 288
-            SF[arr, src : src + 192] = value + got[...].astype(F32)
-            z_push(
-                SF.at[arr, pl.ds(src, 192)],
-                (SF.at[arr, pl.ds(src, CH)], RF.at[arr, pl.ds(src, CH)]),
-                (SF.at[arr, pl.ds(src + CH, CH)], RF.at[arr, pl.ds(src + CH, CH)]),
-                sems[k],
-            )
-            yield
+        value = part(288, 192)
+        arrived(RB.at[arr, pl.ds(0, 192)], sems[1])
+        SB[arr, 288:480] = (value + RB[arr, 288:480].astype(F32)).astype(BF16)
+        push(2, 288, 480, 576)
+        yield
+        value = part(480, 192)
+        arrived(RB.at[arr, pl.ds(0, 192)], sems[2])
+        SF[arr] = value + RB[arr, 480:672].astype(F32)
+        z_push(
+            SF.at[arr],
+            (SF.at[arr, pl.ds(0, CH)], RF.at[arr, pl.ds(0, CH)]),
+            (SF.at[arr, pl.ds(CH, CH)], RF.at[arr, pl.ds(CH, CH)]),
+            sems[3],
+        )
+        yield
         value = part(672, 96)
-        arrived(RF.at[arr, 192:384], sems[3])
-        PRE[arr] = value + RF[arr, 192:288] + RF[arr, 288:384]
+        arrived(RF.at[arr], sems[3])
+        PRE[arr] = value + RF[arr, 0:96] + RF[arr, 96:192]
         yield
 
     def spread(arr):
@@ -595,10 +598,10 @@
             pltpu.VMEM((UNIT, FEAT), BF16),
             pltpu.VMEM((2, 2, 24, HALF), F32),
             pltpu.VMEM((2, 24, HALF), F32),
+            pltpu.VMEM((3, 672, UNIT), BF16),
             pltpu.VMEM((3, 480, UNIT), BF16),
-            pltpu.VMEM((3, 288, UNIT), BF16),
-            pltpu.VMEM((3, 384, UNIT), F32),
-            pltpu.VMEM((3, 384, UNIT), F32),
+            pltpu.VMEM((3, 192, UNIT), F32),
+            pltpu.VMEM((3, 192, UNIT), F32),
             pltpu.VMEM((3, TOK, UNIT), BF16),
             pltpu.VMEM((3, CH, UNIT), F32),
             pltpu.VMEM((672, UNIT), F32),

time: 155 us -> 144 us (0.929)
  Pallas kernels: 147 us -> 136 us
    pallas_call x1, Pallas kernels: 147 us -> 136 us  [per_device(): pl.pallas_call(kernel, out_shape=[pltpu.VMEM((FEAT, UNIT), BF16), pltpu.V...]
where the time goes in v4:
time: 144 us
  Pallas kernels  136 us (94%)
  local copies, waits for them, and re-layouts  4.93 us (3%)
  between operations  3.23 us (2%)
    pallas_call x1, Pallas kernels, per_device(): pl.pallas_call(kernel, out_shape=[pltpu.VMEM((FEAT, UNIT), BF16), pltpu.V...  136 us
    unnamed x4, local copies, waits for them, and re-layouts  4.31 us

profile of v4, /device:TPU:1, one launch (start us, length us, event | category | flops | bytes accessed | tf_op | source)
XLA Modules:
  0.0 144.0 jit_solution(101961005377888248)
XLA Ops:
  3.2 135.9 %shard_map.128 = (bf16[1024,896]{1,0:T(8,128)(2,1)S(1)}, bf16[1024,896]{1,0:T(8,128)(2,1)S(1)}, bf16[896,1024]{1,0:T(8,128)(2,1)S(1)}, bf16[24,1024]{1,0:T(8,128)(2,1)S(1)}, f32[8,128]{1,0:T(8,128)S(1)}) custom-call(f32[1,1]{1,0:T(1,128)S(6)} %copy.22.saved_scale, f32[1,1]{1,0:T(1,128)S(6)} %copy.23.gate_scale, f32[1,1]{1,0:T(1,128)S(6)} %copy.24.up_scale, ...), custom_call_target="tpu_custom_call" | custom-call | tf_op jit(solution)/shard_map/pallas_call | solution.py:581
  139.1 1.2 copy.18
  140.3 0.6 slice_reduce_fusion
  140.9 0.6 copy.21
  141.6 1.2 copy.19
  142.8 1.2 copy.20
